TPU v7x, 512 devices: a whole 4x8x8 slice. The times are simulated.
512 devices in a mesh: rep: 16 (over y_hi, x, core), tp: 32 (over y_lo, z).
Axes of the slice: x: 4, y: 8 (y_hi: 2, y_lo: 4; y = y_hi * 4 + y_lo), z: 8, core: 2. Of those that a mesh axis runs over, the one named last changes fastest.
Arguments:
- queries: bfloat16 [2, 128, 16384], P(None, 'rep', 'tp'), may hold values from -6 to 6
- new_entries: bfloat16 [2, 2, 128, 1024], P(None, None, 'rep'), may hold values from -6 to 6
- kv_cache: bfloat16 [2, 128, 32, 1024], P(None, 'rep'), may hold values from -6 to 6
- residual: bfloat16 [2, 128, 16384], P(None, 'rep', 'tp'), may hold values from -6 to 6
- norm_gain: bfloat16 [16384], P('tp'), may hold values from 0.5 to 1.5
- serving: bfloat16 [16384, 2048], P(None, 'tp'), may hold values from -0.046875 to 0.046875
- sectioning: bfloat16 [16, 16384, 2048], P('rep', 'tp'), may hold values from -0.046875 to 0.046875
- owner_map: int32 [32], replicated, may hold values from 0 to 15, as said below
- lengths: int32 [128], P('rep'), may hold values from 1 to 32, as said below
Outputs:
- next_entries: bfloat16 [2, 128, 2048], P(None, 'rep', 'tp')
Inputs may be any that keep to these rules, and one draw needn't show every extreme that they name: `owner_map`: each of the 16 replicas owns exactly 2 of the 32 row blocks. `lengths`: some row has all 32 positions valid.
All inputs are finite; a program needn't handle non-finite values.
Results may differ from a plain program's by a relative error of at most 0.008.
Values may be sent and summed in bfloat16 or wider, within the bound.
No kernel may reach another device: no remote copies, remote signals or barrier semaphores. Data moves between devices by JAX's collectives and lax.ppermute only.
A program may use at most 64 MiB of HBM per device.

v0:
```python
import jax
import jax.numpy as jnp
from jax import lax
from jax.sharding import PartitionSpec as P

D = 16384
KVH = 8
HD = 128


def spread(block, axis, source):
    block = jnp.where(lax.axis_index(axis) == source, block, jnp.zeros_like(block))
    return lax.psum(block, axis)


def attend_local(queries_here, key_all, value_all, valid, head_width):
    row_count = queries_here.shape[0]
    head_count = queries_here.shape[1] // head_width
    grouped = queries_here.reshape(row_count, head_count, head_width)
    scores = jnp.einsum("rgd,rsd->rgs", grouped, key_all, preferred_element_type=jnp.float32)
    scores = scores / jnp.sqrt(jnp.float32(head_width))
    scores = jnp.where(valid[:, None, :], scores, jnp.float32(-1e30))
    top_score = jnp.max(scores, axis=-1, keepdims=True)
    expd = jnp.exp(scores - top_score)
    weights = (expd / jnp.sum(expd, axis=-1, keepdims=True)).astype(jnp.bfloat16)
    attended = jnp.einsum("rgs,rsd->rgd", weights, value_all, preferred_element_type=jnp.float32)
    return attended.reshape(row_count, head_count * head_width)


def column_product(normed_here, weight_cols):
    return jnp.dot(
        lax.all_gather(normed_here, "tp", axis=1, tiled=True),
        weight_cols,
        preferred_element_type=jnp.float32,
    )


def body(
    queries, new_entries, kv_cache, residual, norm_gain, serving, sectioning, owner_map, lengths
):
    row_count = queries.shape[1]
    cache_span = kv_cache.shape[2]
    group_size = lax.axis_size("tp") // KVH
    kv_head = lax.axis_index("tp") // group_size
    cache_here = lax.dynamic_slice_in_dim(kv_cache, kv_head * HD, HD, 3)
    entries_here = lax.dynamic_slice_in_dim(new_entries, kv_head * HD, HD, 3)
    cached_valid = jnp.arange(cache_span, dtype=jnp.int32)[None, :] < lengths[:, None]
    streams = []
    for step_index in range(2):
        key_rows = [cache_here[0]] + [
            entries_here[earlier, 0][:, None, :] for earlier in range(step_index + 1)
        ]
        value_rows = [cache_here[1]] + [
            entries_here[earlier, 1][:, None, :] for earlier in range(step_index + 1)
        ]
        key_all = jnp.concatenate(key_rows, axis=1)
        value_all = jnp.concatenate(value_rows, axis=1)
        valid = jnp.concatenate(
            [cached_valid, jnp.ones((row_count, step_index + 1), dtype=bool)], axis=1
        )
        attended = attend_local(queries[step_index], key_all, value_all, valid, HD)
        streams.append(residual[step_index].astype(jnp.float32) + attended)
    squares = jnp.stack([jnp.sum(stream * stream, axis=1) for stream in streams])
    totals = lax.psum(squares, "tp")
    gain_here = norm_gain.astype(jnp.float32)
    normed = []
    for step_index in range(2):
        mean_square = totals[step_index][:, None] / jnp.float32(D)
        normed.append(
            (streams[step_index] * lax.rsqrt(mean_square + 1e-05) * gain_here).astype(jnp.bfloat16)
        )
    first = column_product(normed[0], serving).astype(jnp.bfloat16)
    local_rows = sectioning[0]
    owner_here = owner_map[lax.axis_index("tp")]
    fresh_rows = spread(local_rows, "rep", owner_here)
    fresh_cols = lax.all_to_all(fresh_rows, "tp", split_axis=1, concat_axis=0, tiled=True)
    second = column_product(normed[1], fresh_cols).astype(jnp.bfloat16)
    return jnp.stack([first, second])


def solution(mesh):
    placed = (
        P(None, "rep", "tp"),
        P(None, None, "rep", None),
        P(None, "rep", None, None),
        P(None, "rep", "tp"),
        P("tp"),
        P(None, "tp"),
        P("rep", "tp", None),
        P(),
        P("rep"),
    )
    return jax.shard_map(
        body, mesh=mesh, in_specs=placed, out_specs=P(None, "rep", "tp"), check_vma=False
    )
```

profile of v0, /device:TPU:64, one launch (start us, length us, event | category | flops | bytes accessed | tf_op | source)
XLA Modules:
  0.0 498.4 jit_solution(16050089602752986920)
XLA Ops:
  6.5 0.0 copy-start
  6.5 0.0 all-reduce.4.cloned.1.call-start
  6.5 0.0 copy-start.4
  6.5 4.1 copy.40
  10.6 0.0 copy-done.4
  10.6 0.6 dynamic_slice.11
  11.9 1.4 broadcast_select_fusion
  13.3 0.0 all-reduce.4.cloned.1.call-update
  13.3 0.0 copy-start.5
  13.4 0.0 copy-start.3
  13.4 0.0 copy-start.2
  13.4 0.0 copy-start.1
  13.4 196.1 %all-reduce.4.cloned.1.call-done = bf16[512,32,64]{0,2,1:T(8,128)(2,1)} async-done(((bf16[512,32,64]{0,2,1:T(8,128)(2,1)}), bf16[512,32,64]{0,2,1:T(8,128)(2,1)}) %all-reduce.4.cloned.1.call-update) | async-done | bytes 2097168 | tf_op jit(solution)/shard_map/psum | solution.py:13
  209.5 9.5 %all-to-all-start = ((bf16[512,32,64]{0,2,1:T(8,128)(2,1)}), bf16[512,32,64]{0,2,1:T(8,128)(2,1)}, u32[]{:S(2)}, u32[]{:S(2)}) async-start(bf16[512,32,64]{0,2,1:T(8,128)(2,1)} %all-reduce.4.cloned.1.call-done), calls=%async_computation | async-start | bytes 4194304 | tf_op jit(solution)/shard_map/all_to_all | solution.py:76
  219.0 0.0 copy-done.5
  219.0 0.1 iota_compare_fusion
  219.1 0.0 copy-done.3
  219.1 0.7 dynamic-slice_bitcast_fusion.5
  219.9 0.0 copy-done.2
  220.0 0.0 copy-done.1
  220.0 0.9 dynamic-slice_bitcast_fusion.1
  220.9 0.3 fusion.83
  221.2 0.3 fusion.86
  221.6 0.5 multiply_reduce_fusion.1
  222.0 0.5 multiply_reduce_fusion
  222.5 110.8 %psum.14 = f32[2,8]{1,0:T(2,128)S(1)} all-reduce(f32[2,8]{1,0:T(2,128)S(1)} %pad_maximum_fusion.1), channel_id=1, replica_groups=mesh['rep'=16,'tp'=32] {'tp'}, use_global_device_ids=true, to_apply=%region_6.7 | all-reduce | flops 16 | bytes 128 | tf_op jit(solution)/shard_map/psum | solution.py:64
  333.3 0.1 fusion.35
  333.4 80.3 %all_gather.6 = bf16[8,16384]{1,0:T(8,128)(2,1)S(1)} all-gather(bf16[8,512]{1,0:T(8,128)(2,1)S(1)} %get-tuple-element.11), channel_id=1, replica_groups=mesh['rep'=16,'tp'=32] {'tp'}, dimensions={1}, use_global_device_ids=true | all-gather | bytes 270336 | tf_op jit(solution)/shard_map/all_gather | solution.py:32
  413.7 74.2 %all_gather.7 = bf16[8,16384]{1,0:T(8,128)(2,1)S(1)} all-gather(bf16[8,512]{1,0:T(8,128)(2,1)S(1)} %get-tuple-element.12), channel_id=1, replica_groups=mesh['rep'=16,'tp'=32] {'tp'}, dimensions={1}, use_global_device_ids=true | all-gather | bytes 270336 | tf_op jit(solution)/shard_map/all_gather | solution.py:32
  487.9 0.0 copy-done
  487.9 0.6 fusion.10
  488.5 0.0 all-to-all-done
  488.5 1.8 copy.42
  490.3 0.6 fusion.11
  491.0 0.6 pad_maximum_fusion
  (15 shorter events, 0.1 us)
Async XLA Ops:
  6.5 481.3 %copy-start = (bf16[16384,64]{0,1:T(8,128)(2,1)S(1)}, bf16[16384,64]{0,1:T(8,128)(2,1)}, u32[]{:S(2)}) copy-start(bf16[16384,64]{0,1:T(8,128)(2,1)} %param.14) | copy-start | bytes 6291460
  6.5 202.9 %all-reduce.4.cloned.1.call-start = ((), (), s32[]{:S(2)}) async-start(), calls=%async_computation.1 | async-start | bytes 4194304 | tf_op jit(solution)/shard_map/psum | solution.py:13
  6.5 4.1 copy-start.4
  13.3 205.7 %copy-start.5 = (s32[8]{0:T(128)S(1)}, s32[8]{0:T(128)}, u32[]{:S(2)}) copy-start(s32[8]{0:T(128)} %param.17) | copy-start | bytes 100
  13.4 205.8 %copy-start.3 = (bf16[512]{0:T(512)(128)(2,1)S(1)}, bf16[512]{0:T(512)(128)(2,1)}, u32[]{:S(2)}) copy-start(bf16[512]{0:T(512)(128)(2,1)} %param.13) | copy-start | bytes 3076
  13.4 206.6 %copy-start.2 = (bf16[2,8,512]{2,1,0:T(8,128)(2,1)S(1)}, bf16[2,8,512]{2,1,0:T(8,128)(2,1)}, u32[]{:S(2)}) copy-start(bf16[2,8,512]{2,1,0:T(8,128)(2,1)} %param.9) | copy-start | bytes 49156
  13.4 206.6 %copy-start.1 = (bf16[2,8,512]{2,1,0:T(8,128)(2,1)S(1)}, bf16[2,8,512]{2,1,0:T(8,128)(2,1)}, u32[]{:S(2)}) copy-start(bf16[2,8,512]{2,1,0:T(8,128)(2,1)} %param.12) | copy-start | bytes 49156
  209.5 279.1 %all-to-all-start = ((bf16[512,32,64]{0,2,1:T(8,128)(2,1)}), bf16[512,32,64]{0,2,1:T(8,128)(2,1)}, u32[]{:S(2)}, u32[]{:S(2)}) async-start(bf16[512,32,64]{0,2,1:T(8,128)(2,1)} %all-reduce.4.cloned.1.call-done), calls=%async_computation | async-start | bytes 4194304 | tf_op jit(solution)/shard_map/all_to_all | solution.py:76
Sparse Core Ops, SparseCore 0:
  13.5 195.9 all-reduce.3
where the time goes:
time: 498 us
  blocking collectives  265 us (53%)
  waiting for transfers between devices  196 us (39%)
  between operations  14.2 us (3%)
  starting transfers between devices  9.52 us (2%)
  local copies, waits for them, and re-layouts  8.23 us (2%)
    psum x1, waiting for transfers between devices, spread(): return lax.psum(block, axis)  196 us
    all_gather x2, blocking collectives, column_product(): lax.all_gather(normed_here, 'tp', axis=1, tiled=True)  154 us
    psum x1, blocking collectives, body(): totals = lax.psum(squares, 'tp')  111 us
  transfers between devices with their start and end apart: 2, of which 1 were waited for; matrix products, arithmetic and copies ran while one was open for 1% of the time, Pallas kernels for 0%

commit v1 on v0

v1 whole, which is shorter than its diff:
```python
import jax
import jax.numpy as jnp
from jax import lax
from jax.sharding import PartitionSpec as P

D = 16384
KVH = 8
HD = 128
F32 = jnp.float32
BF16 = jnp.bfloat16


def attend_local(queries_here, key_all, value_all, valid, head_width):
    row_count = queries_here.shape[0]
    head_count = queries_here.shape[1] // head_width
    grouped = queries_here.reshape(row_count, head_count, head_width)
    scores = jnp.einsum("rgd,rsd->rgs", grouped, key_all, preferred_element_type=F32)
    scores = scores / jnp.sqrt(F32(head_width))
    scores = jnp.where(valid[:, None, :], scores, F32(-1e30))
    top_score = jnp.max(scores, axis=-1, keepdims=True)
    expd = jnp.exp(scores - top_score)
    weights = (expd / jnp.sum(expd, axis=-1, keepdims=True)).astype(BF16)
    attended = jnp.einsum("rgs,rsd->rgd", weights, value_all, preferred_element_type=F32)
    return attended.reshape(row_count, head_count * head_width)


def exchange(chunks, axis):
    return lax.all_to_all(chunks, axis, split_axis=0, concat_axis=0, tiled=True)


def body(
    queries, new_entries, kv_cache, residual, norm_gain, serving, sectioning, owner_map, lengths
):
    n_rep, n_tp = lax.axis_size("rep"), lax.axis_size("tp")
    row_count, width = queries.shape[1], queries.shape[2]
    cache_span = kv_cache.shape[2]
    kv_head = lax.axis_index("tp") // (n_tp // KVH)
    cache_here = lax.dynamic_slice_in_dim(kv_cache, kv_head * HD, HD, 3)
    entries_here = lax.dynamic_slice_in_dim(new_entries, kv_head * HD, HD, 3)
    cached_valid = jnp.arange(cache_span, dtype=jnp.int32)[None, :] < lengths[:, None]
    gain_here = norm_gain.astype(F32)
    gained, squares = [], []
    for step in range(2):
        key_all, value_all = (
            jnp.concatenate(
                [cache_here[kind]] + [entries_here[e, kind][:, None, :] for e in range(step + 1)],
                axis=1,
            )
            for kind in range(2)
        )
        valid = jnp.concatenate(
            [cached_valid, jnp.ones((row_count, step + 1), dtype=bool)], axis=1
        )
        stream = residual[step].astype(F32) + attend_local(
            queries[step], key_all, value_all, valid, HD
        )
        squares.append(jnp.sum(stream * stream, axis=1))
        gained.append((stream * gain_here).astype(BF16))

    rows_all = exchange(jnp.broadcast_to(gained[1][None], (n_rep, row_count, width)), "rep")
    rows_all = rows_all.reshape(n_rep * row_count, width)
    partial = lax.dot_general(
        sectioning[0], rows_all, (((0,), (1,)), ((), ())), preferred_element_type=F32
    )
    owned = owner_map[lax.axis_index("tp")] == lax.axis_index("rep")
    partial = jnp.where(owned, partial, F32(0)).astype(BF16)
    cols = partial.shape[0] // n_tp
    partial = partial.reshape(n_tp, cols, n_rep * row_count)

    lanes = 128
    tiles = width // lanes
    features = gained[0].reshape(row_count, tiles, lanes).transpose(1, 0, 2)
    features = features.reshape(tiles * row_count, lanes)
    total = jnp.stack(squares, axis=1)
    high = total.astype(BF16)
    low = (total - high.astype(F32)).astype(BF16)
    pieces = jnp.pad(jnp.concatenate([high, low], axis=1), ((0, 8), (0, lanes - 4)))
    extra = jnp.concatenate([features, pieces], axis=0)
    message = jnp.concatenate(
        [partial, jnp.broadcast_to(extra[None], (n_tp,) + extra.shape)], axis=1
    )
    got = exchange(message, "tp")

    summed = jnp.sum(got[:, :cols, :].astype(F32), axis=0)
    mine = exchange(summed.T.astype(BF16).reshape(n_rep, row_count, cols), "rep")
    second = jnp.sum(mine.astype(F32), axis=0)

    square_parts = got[:, cols + tiles * row_count :, :4][:, :row_count, :].astype(F32)
    square_parts = jnp.sum(square_parts, axis=0)
    mean_square = (square_parts[:, :2] + square_parts[:, 2:]) / F32(D)
    scale = lax.rsqrt(mean_square + 1e-05)

    features_all = got[:, cols : cols + tiles * row_count, :]
    features_all = features_all.reshape(n_tp, tiles, row_count, lanes).transpose(2, 0, 1, 3)
    features_all = features_all.reshape(row_count, n_tp * width)
    first = jnp.dot(features_all, serving, preferred_element_type=F32)
    return jnp.stack([first * scale[:, :1], second * scale[:, 1:]]).astype(BF16)


def solution(mesh):
    placed = (
        P(None, "rep", "tp"),
        P(None, None, "rep", None),
        P(None, "rep", None, None),
        P(None, "rep", "tp"),
        P("tp"),
        P(None, "tp"),
        P("rep", "tp", None),
        P(),
        P("rep"),
    )
    return jax.shard_map(
        body, mesh=mesh, in_specs=placed, out_specs=P(None, "rep", "tp"), check_vma=False
    )
```

time: 498 us -> 81.8 us (0.16)
  the two profiles are of different devices: /device:TPU:64 before, /device:TPU:1 now
where the time goes in v1:
time: 81.8 us; the launch traced here: 81.2 us
  blocking collectives  34.6 us (42%)
  starting transfers between devices  17 us (21%)
  waiting for transfers between devices  15.3 us (19%)
  local copies, waits for them, and re-layouts  5.21 us (6%)
  matrix products  4.28 us (5%)
  other arithmetic  4 us (5%)
    all_to_all x1, blocking collectives, exchange(): return lax.all_to_all(chunks, axis, split_axis=0, concat_axis=0, tiled=True)  34.6 us
    all_to_all x2, starting transfers between devices, exchange(): return lax.all_to_all(chunks, axis, split_axis=0, concat_axis=0, tiled=True)  17 us
    all_to_all x2, waiting for transfers between devices, exchange(): return lax.all_to_all(chunks, axis, split_axis=0, concat_axis=0, tiled=True)  15.3 us
    dot_general x1, matrix products, body(): first = jnp.dot(features_all, serving, preferred_element_type=F32)  2.24 us
  transfers between devices with their start and end apart: 2, of which 2 were waited for; matrix products, arithmetic and copies ran while one was open for 5% of the time, Pallas kernels for 0%

profile of v1, /device:TPU:1, one launch (start us, length us, event | category | flops | bytes accessed | tf_op | source)
XLA Modules:
  0.0 81.2 jit_solution(13762052025666993454)
XLA Ops:
  0.0 0.0 copy-start
  0.0 0.0 copy-start.1
  0.0 0.9 %iota_compare_fusion.1 = pred[8,32]{1,0:T(8,128)(4,1)S(1)} fusion(s32[8]{0:T(128)} %param.17), kind=kLoop, calls=%fused_computation.66 | loop fusion | flops 256 | bytes 288 | tf_op jit(solution)/shard_map/lt | solution.py:40
  0.9 0.7 fusion.86
  1.6 0.7 dynamic-slice_bitcast_fusion.5
  2.3 0.7 fusion.85
  3.1 0.7 slice_convert_fusion
  3.8 0.9 %dynamic-slice_bitcast_fusion.1 = (bf16[8,32,128]{2,1,0:T(8,128)(2,1)S(1)}, bf16[8,32,128]{2,1,0:T(8,128)(2,1)S(1)}) fusion(bf16[2,8,32,1024]{3,2,1,0:T(8,128)(2,1)} %param.11, s32[]{:T(128)S(6)} %select_n.38, s32[]{:T(128)S(6)} %add.38), kind=kLoop, calls=%fused_computation.42 | loop fusion | bytes 262152 | tf_op jit(solution)/shard_map/squeeze | solution.py:46
  4.7 0.3 fusion.87
  5.0 0.5 multiply_reduce_fusion
  5.5 0.7 fusion.35
  6.2 0.6 broadcast_in_dim.55
  6.9 11.1 %all-to-all-start = ((bf16[16,8,512]{2,1,0:T(8,128)(2,1)}), bf16[16,8,512]{2,1,0:T(8,128)(2,1)S(1)}, u32[]{:S(2)}, u32[]{:S(2)}) async-start(bf16[16,8,512]{2,1,0:T(8,128)(2,1)} %broadcast_in_dim.55), calls=%async_computation | async-start | bytes 262144 | tf_op jit(solution)/shard_map/all_to_all | solution.py:28
  18.0 0.3 fusion.92
  18.3 0.5 fusion.36
  18.9 0.1 copy.82
  19.0 0.0 copy-done.1
  19.0 0.6 dynamic_slice.9
  20.2 7.8 %all-to-all-done = bf16[16,8,512]{2,1,0:T(8,128)(2,1)S(1)} async-done(((bf16[16,8,512]{2,1,0:T(8,128)(2,1)}), bf16[16,8,512]{2,1,0:T(8,128)(2,1)S(1)}, u32[]{:S(2)}, u32[]{:S(2)}) %all-to-all-start) | async-done | bytes 131104 | tf_op jit(solution)/shard_map/all_to_all | solution.py:28
  28.0 0.0 copy-done
  28.0 0.4 fusion.3
  28.5 0.3 copy.76
  28.7 0.1 broadcast_in_dim.59
  28.8 0.1 pad_maximum_fusion
  28.9 34.6 %all_to_all.15 = bf16[32,112,128]{2,1,0:T(8,128)(2,1)S(1)} all-to-all(bf16[32,112,128]{2,1,0:T(8,128)(2,1)S(1)} %pad_maximum_fusion), channel_id=1, replica_groups=mesh['rep'=16,'tp'=32] {'tp'}, dimensions={0} | all-to-all | bytes 1835008 | tf_op jit(solution)/shard_map/all_to_all | solution.py:28
  63.5 0.1 add_rsqrt_fusion
  63.6 0.2 slice_reduce_fusion.2
  63.8 0.1 slice_reduce_fusion
  63.9 0.1 copy.81
  64.0 0.7 reshape.96
  64.7 5.9 %all-to-all-start.2 = ((bf16[16,2,256]{2,1,0:T(2,128)(2,1)}), bf16[16,2,256]{2,1,0:T(2,128)(2,1)S(1)}, u32[]{:S(2)}, u32[]{:S(2)}) async-start(bf16[16,2,256]{2,1,0:T(2,128)(2,1)} %reshape.96), calls=%async_computation.2 | async-start | bytes 32768 | tf_op jit(solution)/shard_map/all_to_all | solution.py:28
  70.7 2.2 %fusion.14 = bf16[1,8,64]{2,1,0:T(8,128)(2,1)S(1)} fusion(bf16[8,16384]{1,0:T(8,128)(2,1)S(1)} %bitcast.81, bf16[16384,64]{0,1:T(8,128)(2,1)} %param.14, f32[8]{0:T(128)S(1)} %get-tuple-element.5), kind=kOutput, calls=%fused_computation.19 | convolution fusion | flops 16778240 | bytes 2360352 | tf_op jit(solution)/shard_map/dot_general | solution.py:96
  72.9 7.5 %all-to-all-done.2 = bf16[16,2,256]{2,1,0:T(2,128)(2,1)S(1)} async-done(((bf16[16,2,256]{2,1,0:T(2,128)(2,1)}), bf16[16,2,256]{2,1,0:T(2,128)(2,1)S(1)}, u32[]{:S(2)}, u32[]{:S(2)}) %all-to-all-start.2) | async-done | bytes 16416 | tf_op jit(solution)/shard_map/all_to_all | solution.py:28
  80.4 0.1 reshape.97
  80.5 0.1 fusion.39
  80.6 0.6 pad_maximum_fusion.1
  (19 shorter events, 0.2 us)
Async XLA Ops:
  0.0 28.0 %copy-start = (bf16[1,512,2048]{2,1,0:T(8,128)(2,1)S(1)}, bf16[1,512,2048]{2,1,0:T(8,128)(2,1)}, u32[]{:S(2)}) copy-start(bf16[1,512,2048]{2,1,0:T(8,128)(2,1)} %param.15) | copy-start | bytes 6291460
  0.0 19.0 %copy-start.1 = (s32[32]{0:T(128)S(1)}, s32[32]{0:T(128)}, u32[]{:S(2)}) copy-start(s32[32]{0:T(128)} %param.16) | copy-start | bytes 388
  6.9 21.1 %all-to-all-start = ((bf16[16,8,512]{2,1,0:T(8,128)(2,1)}), bf16[16,8,512]{2,1,0:T(8,128)(2,1)S(1)}, u32[]{:S(2)}, u32[]{:S(2)}) async-start(bf16[16,8,512]{2,1,0:T(8,128)(2,1)} %broadcast_in_dim.55), calls=%async_computation | async-start | bytes 262144 | tf_op jit(solution)/shard_map/all_to_all | solution.py:28
  64.7 15.7 %all-to-all-start.2 = ((bf16[16,2,256]{2,1,0:T(2,128)(2,1)}), bf16[16,2,256]{2,1,0:T(2,128)(2,1)S(1)}, u32[]{:S(2)}, u32[]{:S(2)}) async-start(bf16[16,2,256]{2,1,0:T(2,128)(2,1)} %reshape.96), calls=%async_computation.2 | async-start | bytes 32768 | tf_op jit(solution)/shard_map/all_to_all | solution.py:28

commit v2 on v0

v2 whole, which is shorter than its diff:
```python
import jax
import jax.numpy as jnp
from jax import lax
from jax.experimental import pallas as pl
from jax.experimental.pallas import tpu as pltpu
from jax.sharding import PartitionSpec as P

D = 16384
KVH = 8
HD = 128
F32 = jnp.float32
BF16 = jnp.bfloat16
NT = (((1,), (1,)), ((), ()))


def exchange(chunks, axis, groups=None):
    return lax.all_to_all(
        chunks, axis, split_axis=0, concat_axis=0, axis_index_groups=groups, tiled=True
    )


def attend_kernel(head_ref, lengths_ref, q_ref, e_ref, kv_ref, res_ref, gain_ref, send_ref, extra_ref):
    rows, span = kv_ref.shape[1], kv_ref.shape[2]
    tiles = q_ref.shape[2] // HD
    cached = rows * span
    n_keys = cached + 2 * rows
    n_queries = 2 * tiles * rows

    def stacked(value):
        return jnp.concatenate([value[:, t * HD : (t + 1) * HD] for t in range(tiles)], axis=0)

    query = jnp.concatenate([stacked(q_ref[s].astype(F32)) for s in range(2)], axis=0).astype(BF16)

    def keys(kind):
        fresh = jnp.concatenate([e_ref[s, kind].astype(F32) for s in range(2)], axis=0)
        return jnp.concatenate([kv_ref[kind].reshape(cached, HD), fresh.astype(BF16)], axis=0)

    scores = lax.dot_general(query, keys(0), NT, preferred_element_type=F32)
    scores = scores / jnp.sqrt(F32(HD))
    column = lax.broadcasted_iota(jnp.int32, (n_queries, n_keys), 1)
    line = lax.broadcasted_iota(jnp.int32, (n_queries, n_keys), 0)
    old = column < cached
    row_of_key = jnp.where(old, lax.div(column, span), lax.rem(column, rows))
    limit = jnp.zeros_like(column)
    for r in range(rows):
        limit = jnp.where(row_of_key == r, lengths_ref[r], limit)
    late = jnp.where(column < cached + rows, 0, tiles * rows)
    bar = jnp.where(old, lax.rem(column, span), late)
    against = jnp.where(old, limit - 1, line)
    seen = (bar <= against) & (row_of_key == lax.rem(line, rows))
    scores = jnp.where(seen, scores, F32(-1e30))
    top = jnp.max(scores, axis=1, keepdims=True)
    expd = jnp.exp(scores - top)
    weights = (expd / jnp.sum(expd, axis=1, keepdims=True)).astype(BF16)
    attended = jnp.dot(weights, keys(1), preferred_element_type=F32)

    lane = lax.broadcasted_iota(jnp.int32, (rows, HD), 1)
    pieces = jnp.zeros((rows, HD), F32)
    gain = gain_ref[...].astype(F32)
    for s in range(2):
        base = s * tiles * rows
        there = jnp.concatenate(
            [attended[base + t * rows : base + (t + 1) * rows] for t in range(tiles)], axis=1
        )
        stream = res_ref[s].astype(F32) + there
        square = jnp.sum(stream * stream, axis=1, keepdims=True)
        high = square.astype(BF16).astype(F32)
        pieces = jnp.where(lane == s, high, jnp.where(lane == 2 + s, square - high, pieces))
        gained = stream * gain
        if s == 0:
            first = stacked(gained)
        else:
            gained = gained.astype(BF16)
            for p in range(send_ref.shape[0]):
                send_ref[p] = gained
    extra_ref[...] = jnp.concatenate([first, pieces], axis=0).astype(BF16)


def product_kernel(pick_ref, rows_ref, mine_ref, peer_ref, extra_ref, out_ref):
    n_tp = out_ref.shape[0]
    cols = mine_ref.shape[2] // n_tp
    chips, per, width = rows_ref.shape
    count = chips * per
    half = count // 2
    low = lax.broadcasted_iota(jnp.int32, (half, 2 * cols), 1) < cols
    extra = extra_ref[...].astype(F32)

    def fill(weight_ref):
        rows = rows_ref[...].astype(F32).reshape(count, width).astype(BF16)
        step = 512
        for start in range(0, n_tp * cols, step):
            part = jnp.dot(
                rows, weight_ref[0, :, start : start + step], preferred_element_type=F32
            )
            for j in range(step // (2 * cols)):
                tile = part[:, j * 2 * cols : (j + 1) * 2 * cols]
                turned = pltpu.roll(tile, cols, 1)
                even = jnp.where(low, tile[:half], turned[half:])
                odd = jnp.where(low, turned[:half], tile[half:])
                at = start // cols + 2 * j
                out_ref[at] = jnp.concatenate([even, extra], axis=0).astype(BF16)
                out_ref[at + 1] = jnp.concatenate([odd, extra], axis=0).astype(BF16)

    pick = pick_ref[0]

    @pl.when(pick == 0)
    def _():
        fill(mine_ref)

    @pl.when(pick == 1)
    def _():
        fill(peer_ref)

    @pl.when(pick > 1)
    def _():
        empty = jnp.concatenate([jnp.zeros((half, 2 * cols), F32), extra], axis=0).astype(BF16)
        for at in range(n_tp):
            out_ref[at] = empty


def attend(head, lengths, queries, entries, cache, residual, gain, n_chips):
    _, rows, width = queries.shape
    span = cache.shape[2]
    tiles = width // HD
    whole = lambda *shape: pl.BlockSpec(shape, lambda i, *_: (0,) * len(shape))
    by_head = lambda *shape: pl.BlockSpec(
        shape, lambda i, head_ref, _: (0,) * (len(shape) - 1) + (head_ref[0],)
    )
    return pl.pallas_call(
        attend_kernel,
        grid_spec=pltpu.PrefetchScalarGridSpec(
            num_scalar_prefetch=2,
            grid=(1,),
            in_specs=[
                whole(2, rows, width),
                by_head(2, 2, rows, HD),
                by_head(2, rows, span, HD),
                whole(2, rows, width),
                whole(1, width),
            ],
            out_specs=[whole(n_chips, rows, width), whole((tiles + 1) * rows, HD)],
        ),
        out_shape=[
            jax.ShapeDtypeStruct((n_chips, rows, width), BF16),
            jax.ShapeDtypeStruct(((tiles + 1) * rows, HD), BF16),
        ],
        compiler_params=pltpu.CompilerParams(vmem_limit_bytes=16 * 2**20),
        cost_estimate=pl.CostEstimate(flops=10**7, bytes_accessed=300_000, transcendentals=20_000),
    )(head, lengths, queries, entries, cache, residual, gain)


def product(pick, rows_all, mine, peer, extra, n_tp):
    vmem = pl.BlockSpec(memory_space=pltpu.VMEM)
    chips, per, _ = rows_all.shape
    cols = mine.shape[2] // n_tp
    lines = chips * per // 2 + extra.shape[0]
    return pl.pallas_call(
        product_kernel,
        in_specs=[pl.BlockSpec(memory_space=pltpu.SMEM), vmem, vmem, vmem, vmem],
        out_specs=vmem,
        out_shape=jax.ShapeDtypeStruct((n_tp, lines, 2 * cols), BF16),
        compiler_params=pltpu.CompilerParams(vmem_limit_bytes=16 * 2**20),
        cost_estimate=pl.CostEstimate(flops=13 * 10**7, bytes_accessed=3_000_000, transcendentals=0),
    )(pick, rows_all, mine, peer, extra)


def body(
    queries, new_entries, kv_cache, residual, norm_gain, serving, sectioning, owner_map, lengths
):
    n_rep, n_tp = lax.axis_size("rep"), lax.axis_size("tp")
    n_chips = n_rep // 2
    row_count, width = queries.shape[1], queries.shape[2]
    rep, tp = lax.axis_index("rep"), lax.axis_index("tp")
    kv_head = (tp // (n_tp // KVH)).astype(jnp.int32).reshape(1)
    send, extra = attend(
        kv_head, lengths, queries, new_entries, kv_cache, residual, norm_gain[None], n_chips
    )

    same_core = [[i for i in range(n_rep) if i % 2 == core] for core in range(2)]
    rows_all = exchange(send, "rep", same_core)
    peer_rows = lax.ppermute(sectioning, "rep", [(i, i ^ 1) for i in range(n_rep)])
    owner = owner_map[tp]
    pick = jnp.where(owner == rep, 0, jnp.where(owner == (rep ^ 1), 1, 2))
    message = product(
        pick.astype(jnp.int32).reshape(1), rows_all, sectioning, peer_rows, extra, n_tp
    )

    half = n_chips * row_count // 2
    tiles = width // HD
    got = exchange(message, "tp")
    cols = sectioning.shape[2] // n_tp
    summed = jnp.sum(got[:, :half].astype(F32), axis=0).astype(BF16)
    summed = summed.reshape(n_chips // 2, row_count, 2 * cols)
    mine = exchange(jnp.concatenate([summed, summed], axis=0), "rep", same_core)
    second = jnp.sum(mine.astype(F32), axis=0)
    second = jnp.where(rep // 2 < n_chips // 2, second[:, :cols], second[:, cols:])

    parts = jnp.sum(got[:, half + tiles * row_count :, :4].astype(F32), axis=0)
    mean_square = (parts[:, :2] + parts[:, 2:]) / F32(D)
    scale = lax.rsqrt(mean_square + 1e-05)
    features = got[:, half : half + tiles * row_count].reshape(n_tp, tiles, row_count, HD)
    features = features.transpose(2, 0, 1, 3).reshape(row_count, n_tp * width)
    first = jnp.dot(features, serving, preferred_element_type=F32)
    return jnp.stack([first * scale[:, :1], second * scale[:, 1:]]).astype(BF16)


def solution(mesh):
    placed = (
        P(None, "rep", "tp"),
        P(None, None, "rep", None),
        P(None, "rep", None, None),
        P(None, "rep", "tp"),
        P("tp"),
        P(None, "tp"),
        P("rep", "tp", None),
        P(),
        P("rep"),
    )
    return jax.shard_map(
        body, mesh=mesh, in_specs=placed, out_specs=P(None, "rep", "tp"), check_vma=False
    )
```

time: 498 us -> 77.2 us (0.16)
  blocking collectives: 265 us -> 0 us
  waiting for transfers between devices: 196 us -> 35.2 us
  starting transfers between devices: 9.52 us -> 25.9 us
  between operations: 14.2 us -> 1.39 us
    psum x1 -> x0, waiting for transfers between devices: 196 us -> none  [spread(): return lax.psum(block, axis)]
    all_gather x2 -> x0, blocking collectives: 154 us -> none  [column_product(): lax.all_gather(normed_here, 'tp', axis=1, tiled=True)]
    psum x1 -> x0, blocking collectives: 111 us -> none  [body(): totals = lax.psum(squares, 'tp')]
    all_to_all x1 -> x3, waiting for transfers between devices: 0.01 us -> 35.2 us  [exchange(): lax.all_to_all(chunks, axis, split_axis=0, concat_axis=0, axis_index_grou...]
    all_to_all x1 -> x3, starting transfers between devices: 9.52 us -> 23.8 us  [exchange(): lax.all_to_all(chunks, axis, split_axis=0, concat_axis=0, axis_index_grou...]
  transfers between devices with their start and end apart: 2 -> 4, of which waited for: 1 -> 3; matrix products, arithmetic and copies ran while one was open for 1% -> 3% of each run, Pallas kernels for 0% -> 2%
where the time goes in v2:
time: 77.2 us; the launch traced here: 76.6 us
  waiting for transfers between devices  35.2 us (46%)
  starting transfers between devices  25.9 us (34%)
  local copies, waits for them, and re-layouts  7.85 us (10%)
  Pallas kernels  4.16 us (5%)
  other arithmetic  1.46 us (2%)
  between operations  1.39 us (2%)
    all_to_all x3, waiting for transfers between devices, exchange(): lax.all_to_all(chunks, axis, split_axis=0, concat_axis=0, axis_index_grou...  35.2 us
    all_to_all x3, starting transfers between devices, exchange(): lax.all_to_all(chunks, axis, split_axis=0, concat_axis=0, axis_index_grou...  23.8 us
    unnamed x14, local copies, waits for them, and re-layouts  5.75 us
    pallas_call x1, Pallas kernels, product(): pl.pallas_call(product_kernel, in_specs=[pl.BlockSpec(memory_space=pltpu....  2.5 us
    ppermute x1, starting transfers between devices, body(): lax.ppermute(sectioning, 'rep', [(i, i ^ 1) for i in range(n_rep)])  2.04 us
    pallas_call x1, Pallas kernels, attend(): pl.pallas_call(attend_kernel, grid_spec=pltpu.PrefetchScalarGridSpec(num_...  1.66 us
  transfers between devices with their start and end apart: 4, of which 3 were waited for; matrix products, arithmetic and copies ran while one was open for 3% of the time, Pallas kernels for 2%

profile of v2, /device:TPU:64, one launch (start us, length us, event | category | flops | bytes accessed | tf_op | source)
XLA Modules:
  0.0 76.6 jit_solution(11890434867498273417)
XLA Ops:
  0.0 0.0 copy-start
  0.0 2.0 %collective-permute-start = (bf16[1,512,2048]{2,1,0:T(8,128)(2,1)}, bf16[1,512,2048]{2,1,0:T(8,128)(2,1)}, u32[]{:S(2)}, u32[]{:S(2)}) collective-permute-start(bf16[1,512,2048]{2,1,0:T(8,128)(2,1)} %mine_ref.1), channel_id=1, source_target_pairs={{0,32},{32,0},{64,96},{96,64},{128,160},{160,128},{192,224},{224,1... | collective-permute-start | bytes 6291464 | tf_op jit(solution)/shard_map/ppermute | solution.py:181
  2.1 0.7 broadcast_in_dim.3.gain_ref
  2.7 0.0 copy-start.2
  2.8 1.2 %copy-done.2 = bf16[2,8,32,1024]{3,2,1,0:T(8,128)(2,1)S(1)} copy-done((bf16[2,8,32,1024]{3,2,1,0:T(8,128)(2,1)S(1)}, bf16[2,8,32,1024]{3,2,1,0:T(8,128)(2,1)}, u32[]{:S(2)}) %copy-start.2) | copy-done | bytes 1048600
  4.0 0.0 copy-start.3
  4.0 0.8 %copy-done.3 = bf16[2,2,8,1024]{3,2,1,0:T(8,128)(2,1)S(1)} copy-done((bf16[2,2,8,1024]{3,2,1,0:T(8,128)(2,1)S(1)}, bf16[2,2,8,1024]{3,2,1,0:T(8,128)(2,1)}, u32[]{:S(2)}) %copy-start.3) | copy-done | bytes 65560
  4.8 0.0 copy-start.4
  4.8 0.7 copy-done.4
  5.5 0.0 copy-start.5
  5.5 0.7 copy-done.5
  6.2 0.0 copy-start.6
  6.3 0.7 copy-done.6
  6.9 1.7 %shard_map.91 = (bf16[8,8,512]{2,1,0:T(8,128)(2,1)}, bf16[40,128]{1,0:T(8,128)(2,1)S(1)}) custom-call(s32[1]{0:T(128)} %bitcast.2.head_ref, s32[8]{0:T(128)S(1)} %copy-done.6, bf16[2,8,512]{2,1,0:T(8,128)(2,1)S(1)} %copy-done.4, bf16[2,2,8,1024]{3,2,1,0:T(8,128)(2,1)S(1)} %copy-done.3, bf16[2,8,32,1024]{3,2,1,0:T(8,128)(2,1)S(1)} %copy-done.2, ...), custom_call_target="tpu_custom_call" | custom-call | flops 10000000 | bytes 300000 | tf_op jit(solution)/shard_map/pallas_call | solution.py:129
  8.6 9.6 %all-to-all-start = ((bf16[8,8,512]{2,1,0:T(8,128)(2,1)}), bf16[8,8,512]{2,1,0:T(8,128)(2,1)S(1)}, u32[]{:S(2)}, u32[]{:S(2)}) async-start(bf16[8,8,512]{2,1,0:T(8,128)(2,1)} %get-tuple-element.7), calls=%async_computation | async-start | bytes 131072 | tf_op jit(solution)/shard_map/all_to_all | solution.py:17
  18.1 1.2 %dynamic_slice.3 = s32[1]{0:T(128)} dynamic-slice(s32[32]{0:T(128)} %param.16, s32[]{:T(128)S(6)} %select_n.27), dynamic_slice_sizes={1} | dynamic-slice | bytes 12 | tf_op jit(solution)/shard_map/dynamic_slice | solution.py:182
  20.7 7.7 %all-to-all-done.rows_ref = bf16[8,8,512]{2,1,0:T(8,128)(2,1)S(1)} async-done(((bf16[8,8,512]{2,1,0:T(8,128)(2,1)}), bf16[8,8,512]{2,1,0:T(8,128)(2,1)S(1)}, u32[]{:S(2)}, u32[]{:S(2)}) %all-to-all-start) | async-done | bytes 65568 | tf_op jit(solution)/shard_map/all_to_all | solution.py:17
  28.4 0.0 collective-permute-done.peer_ref
  28.4 0.0 copy-start.1
  28.4 1.6 %copy-done.1 = bf16[1,512,2048]{2,1,0:T(8,128)(2,1)S(1)} copy-done((bf16[1,512,2048]{2,1,0:T(8,128)(2,1)S(1)}, bf16[1,512,2048]{2,1,0:T(8,128)(2,1)}, u32[]{:S(2)}) %copy-start.1) | copy-done | bytes 2097176
  30.0 2.5 %shard_map.92 = bf16[32,72,128]{2,1,0:T(8,128)(2,1)} custom-call(s32[1]{0:T(128)} %bitcast.1.pick_ref, bf16[8,8,512]{2,1,0:T(8,128)(2,1)S(1)} %all-to-all-done.rows_ref, bf16[1,512,2048]{2,1,0:T(8,128)(2,1)S(1)} %copy-done.1, bf16[1,512,2048]{2,1,0:T(8,128)(2,1)} %collective-permute-done.peer_ref, bf16[40,128]{1,0:T(8,128)(2,1)S(1)} %get-tuple-element.8.extra_ref), custom_call_target="tpu_custom_call" | custom-call | flops 130000000 | bytes 3000000 | tf_op jit(solution)/shard_map/pallas_call | solution.py:157
  32.5 11.0 %all-to-all-start.1 = ((bf16[32,72,128]{2,1,0:T(8,128)(2,1)}), bf16[32,72,128]{2,1,0:T(8,128)(2,1)S(1)}, u32[]{:S(2)}, u32[]{:S(2)}) async-start(bf16[32,72,128]{2,1,0:T(8,128)(2,1)} %shard_map.92), calls=%async_computation.1 | async-start | bytes 1179648 | tf_op jit(solution)/shard_map/all_to_all | solution.py:17
  43.5 18.1 %all-to-all-done.1 = bf16[32,72,128]{2,1,0:T(8,128)(2,1)S(1)} async-done(((bf16[32,72,128]{2,1,0:T(8,128)(2,1)}), bf16[32,72,128]{2,1,0:T(8,128)(2,1)S(1)}, u32[]{:S(2)}, u32[]{:S(2)}) %all-to-all-start.1) | async-done | bytes 589856 | tf_op jit(solution)/shard_map/all_to_all | solution.py:17
  61.6 0.1 add_rsqrt_fusion
  61.6 0.2 slice_reduce_fusion.2
  61.8 0.1 fusion.3
  61.9 0.6 pad_maximum_fusion
  62.5 3.3 %all-to-all-start.2 = ((bf16[8,8,128]{2,1,0:T(8,128)(2,1)}), bf16[8,8,128]{2,1,0:T(8,128)(2,1)S(1)}, u32[]{:S(2)}, u32[]{:S(2)}) async-start(bf16[8,8,128]{2,1,0:T(8,128)(2,1)} %pad_maximum_fusion), calls=%async_computation.2 | async-start | bytes 32768 | tf_op jit(solution)/shard_map/all_to_all | solution.py:17
  65.8 0.0 copy-done
  65.8 0.6 fusion.1
  66.5 9.4 %all-to-all-done.2 = bf16[8,8,128]{2,1,0:T(8,128)(2,1)S(1)} async-done(((bf16[8,8,128]{2,1,0:T(8,128)(2,1)}), bf16[8,8,128]{2,1,0:T(8,128)(2,1)S(1)}, u32[]{:S(2)}, u32[]{:S(2)}) %all-to-all-start.2) | async-done | bytes 16416 | tf_op jit(solution)/shard_map/all_to_all | solution.py:17
  75.9 0.1 fusion.2
  76.0 0.6 pad_maximum_fusion.1
  (2 shorter events, 0.0 us)
Async XLA Ops:
  0.0 65.8 %copy-start = (bf16[16384,64]{0,1:T(8,128)(2,1)S(1)}, bf16[16384,64]{0,1:T(8,128)(2,1)}, u32[]{:S(2)}) copy-start(bf16[16384,64]{0,1:T(8,128)(2,1)} %param.14) | copy-start | bytes 6291460
  0.0 28.4 %collective-permute-start = (bf16[1,512,2048]{2,1,0:T(8,128)(2,1)}, bf16[1,512,2048]{2,1,0:T(8,128)(2,1)}, u32[]{:S(2)}, u32[]{:S(2)}) collective-permute-start(bf16[1,512,2048]{2,1,0:T(8,128)(2,1)} %mine_ref.1), channel_id=1, source_target_pairs={{0,32},{32,0},{64,96},{96,64},{128,160},{160,128},{192,224},{224,1... | collective-permute-start | bytes 6291464 | tf_op jit(solution)/shard_map/ppermute | solution.py:181
  2.7 1.2 %copy-start.2 = (bf16[2,8,32,1024]{3,2,1,0:T(8,128)(2,1)S(1)}, bf16[2,8,32,1024]{3,2,1,0:T(8,128)(2,1)}, u32[]{:S(2)}) copy-start(bf16[2,8,32,1024]{3,2,1,0:T(8,128)(2,1)} %kv_ref.1) | copy-start | bytes 3145732
  4.0 0.8 %copy-start.3 = (bf16[2,2,8,1024]{3,2,1,0:T(8,128)(2,1)S(1)}, bf16[2,2,8,1024]{3,2,1,0:T(8,128)(2,1)}, u32[]{:S(2)}) copy-start(bf16[2,2,8,1024]{3,2,1,0:T(8,128)(2,1)} %e_ref.1) | copy-start | bytes 196612
  4.8 0.7 copy-start.4
  5.5 0.7 copy-start.5
  6.2 0.7 copy-start.6
  8.6 19.8 %all-to-all-start = ((bf16[8,8,512]{2,1,0:T(8,128)(2,1)}), bf16[8,8,512]{2,1,0:T(8,128)(2,1)S(1)}, u32[]{:S(2)}, u32[]{:S(2)}) async-start(bf16[8,8,512]{2,1,0:T(8,128)(2,1)} %get-tuple-element.7), calls=%async_computation | async-start | bytes 131072 | tf_op jit(solution)/shard_map/all_to_all | solution.py:17
  28.4 1.6 %copy-start.1 = (bf16[1,512,2048]{2,1,0:T(8,128)(2,1)S(1)}, bf16[1,512,2048]{2,1,0:T(8,128)(2,1)}, u32[]{:S(2)}) copy-start(bf16[1,512,2048]{2,1,0:T(8,128)(2,1)} %mine_ref.1) | copy-start | bytes 6291460
  32.5 29.0 %all-to-all-start.1 = ((bf16[32,72,128]{2,1,0:T(8,128)(2,1)}), bf16[32,72,128]{2,1,0:T(8,128)(2,1)S(1)}, u32[]{:S(2)}, u32[]{:S(2)}) async-start(bf16[32,72,128]{2,1,0:T(8,128)(2,1)} %shard_map.92), calls=%async_computation.1 | async-start | bytes 1179648 | tf_op jit(solution)/shard_map/all_to_all | solution.py:17
  62.5 13.4 %all-to-all-start.2 = ((bf16[8,8,128]{2,1,0:T(8,128)(2,1)}), bf16[8,8,128]{2,1,0:T(8,128)(2,1)S(1)}, u32[]{:S(2)}, u32[]{:S(2)}) async-start(bf16[8,8,128]{2,1,0:T(8,128)(2,1)} %pad_maximum_fusion), calls=%async_computation.2 | async-start | bytes 32768 | tf_op jit(solution)/shard_map/all_to_all | solution.py:17

commit v3 on v2

--- a/solution.py
+++ b/solution.py
@@ -19,7 +19,27 @@
     )
 
 
-def attend_kernel(head_ref, lengths_ref, q_ref, e_ref, kv_ref, res_ref, gain_ref, send_ref, extra_ref):
+def attend_kernel(
+    lengths_hbm, q_hbm, e_hbm, kv_hbm, res_hbm, gain_hbm, send_ref, extra_ref,
+    lengths_ref, q_ref, e_ref, kv_ref, res_ref, gain_ref, sems,
+):
+    head = lax.div(lax.axis_index("tp"), lax.div(lax.axis_size("tp"), KVH))
+    columns = pl.ds(pl.multiple_of(head * HD, HD), HD)
+    copies = [
+        pltpu.make_async_copy(source, target, sems.at[i])
+        for i, (source, target) in enumerate(
+            [
+                (kv_hbm.at[:, :, :, columns], kv_ref),
+                (e_hbm.at[:, :, :, columns], e_ref),
+                (q_hbm, q_ref),
+                (lengths_hbm, lengths_ref),
+                (res_hbm, res_ref),
+                (gain_hbm, gain_ref),
+            ]
+        )
+    ]
+    for copy in copies:
+        copy.start()
     rows, span = kv_ref.shape[1], kv_ref.shape[2]
     tiles = q_ref.shape[2] // HD
     cached = rows * span
@@ -29,18 +49,19 @@
     def stacked(value):
         return jnp.concatenate([value[:, t * HD : (t + 1) * HD] for t in range(tiles)], axis=0)
 
-    query = jnp.concatenate([stacked(q_ref[s].astype(F32)) for s in range(2)], axis=0).astype(BF16)
-
     def keys(kind):
         fresh = jnp.concatenate([e_ref[s, kind].astype(F32) for s in range(2)], axis=0)
         return jnp.concatenate([kv_ref[kind].reshape(cached, HD), fresh.astype(BF16)], axis=0)
 
-    scores = lax.dot_general(query, keys(0), NT, preferred_element_type=F32)
-    scores = scores / jnp.sqrt(F32(HD))
     column = lax.broadcasted_iota(jnp.int32, (n_queries, n_keys), 1)
     line = lax.broadcasted_iota(jnp.int32, (n_queries, n_keys), 0)
     old = column < cached
     row_of_key = jnp.where(old, lax.div(column, span), lax.rem(column, rows))
+    for copy in copies:
+        copy.wait()
+    query = jnp.concatenate([stacked(q_ref[s].astype(F32)) for s in range(2)], axis=0).astype(BF16)
+    scores = lax.dot_general(query, keys(0), NT, preferred_element_type=F32)
+    scores = scores / jnp.sqrt(F32(HD))
     limit = jnp.zeros_like(column)
     for r in range(rows):
         limit = jnp.where(row_of_key == r, lengths_ref[r], limit)
@@ -56,7 +77,7 @@
 
     lane = lax.broadcasted_iota(jnp.int32, (rows, HD), 1)
     pieces = jnp.zeros((rows, HD), F32)
-    gain = gain_ref[...].astype(F32)
+    gain = gain_ref[...].astype(F32)[None]
     for s in range(2):
         base = s * tiles * rows
         there = jnp.concatenate(
@@ -76,90 +97,137 @@
     extra_ref[...] = jnp.concatenate([first, pieces], axis=0).astype(BF16)
 
 
-def product_kernel(pick_ref, rows_ref, mine_ref, peer_ref, extra_ref, out_ref):
+def product_kernel(
+    pick_ref, rows_hbm, mine_hbm, peer_hbm, extra_hbm, out_hbm,
+    rows_ref, extra_ref, weight_ref, out_ref, in_sems, out_sems,
+):
     n_tp = out_ref.shape[0]
-    cols = mine_ref.shape[2] // n_tp
+    cols = mine_hbm.shape[2] // n_tp
     chips, per, width = rows_ref.shape
     count = chips * per
     half = count // 2
-    low = lax.broadcasted_iota(jnp.int32, (half, 2 * cols), 1) < cols
+    n_steps, _, step = weight_ref.shape
+    each = n_tp // n_steps
+    pick = pick_ref[0]
+
+    def fetch(source, i):
+        return pltpu.make_async_copy(
+            source.at[0, :, pl.ds(i * step, step)], weight_ref.at[i], in_sems.at[i]
+        )
+
+    def ship(i):
+        part = pl.ds(i * each, each)
+        return pltpu.make_async_copy(out_ref.at[part], out_hbm.at[part], out_sems.at[i])
+
+    small = [
+        pltpu.make_async_copy(extra_hbm, extra_ref, in_sems.at[n_steps]),
+        pltpu.make_async_copy(rows_hbm, rows_ref, in_sems.at[n_steps + 1]),
+    ]
+    for copy in small:
+        copy.start()
+
+    @pl.when(pick == 0)
+    def _():
+        for i in range(n_steps):
+            fetch(mine_hbm, i).start()
+
+    @pl.when(pick == 1)
+    def _():
+        for i in range(n_steps):
+            fetch(peer_hbm, i).start()
+
+    for copy in small:
+        copy.wait()
     extra = extra_ref[...].astype(F32)
 
-    def fill(weight_ref):
-        rows = rows_ref[...].astype(F32).reshape(count, width).astype(BF16)
-        step = 512
-        for start in range(0, n_tp * cols, step):
-            part = jnp.dot(
-                rows, weight_ref[0, :, start : start + step], preferred_element_type=F32
-            )
-            for j in range(step // (2 * cols)):
+    @pl.when(pick < 2)
+    def _():
+        low = lax.broadcasted_iota(jnp.int32, (half, 2 * cols), 1) < cols
+        rows = rows_ref[...].reshape(count, width)
+
+        def one(i, carry):
+            fetch(mine_hbm, i).wait()
+            part = jnp.dot(rows, weight_ref[i], preferred_element_type=F32)
+            for j in range(each // 2):
                 tile = part[:, j * 2 * cols : (j + 1) * 2 * cols]
                 turned = pltpu.roll(tile, cols, 1)
                 even = jnp.where(low, tile[:half], turned[half:])
                 odd = jnp.where(low, turned[:half], tile[half:])
-                at = start // cols + 2 * j
+                at = i * each + 2 * j
                 out_ref[at] = jnp.concatenate([even, extra], axis=0).astype(BF16)
                 out_ref[at + 1] = jnp.concatenate([odd, extra], axis=0).astype(BF16)
-
-    pick = pick_ref[0]
-
-    @pl.when(pick == 0)
-    def _():
-        fill(mine_ref)
-
-    @pl.when(pick == 1)
-    def _():
-        fill(peer_ref)
+            ship(i).start()
+            return carry
+
+        lax.fori_loop(0, n_steps, one, 0)
 
     @pl.when(pick > 1)
     def _():
         empty = jnp.concatenate([jnp.zeros((half, 2 * cols), F32), extra], axis=0).astype(BF16)
-        for at in range(n_tp):
+
+        def one(at, carry):
             out_ref[at] = empty
-
-
-def attend(head, lengths, queries, entries, cache, residual, gain, n_chips):
+            return carry
+
+        lax.fori_loop(0, n_tp, one, 0)
+        for i in range(n_steps):
+            ship(i).start()
+
+    for i in range(n_steps):
+        ship(i).wait()
+
+
+VMEM_SPEC = pl.BlockSpec(memory_space=pltpu.VMEM)
+HBM_SPEC = pl.BlockSpec(memory_space=pltpu.HBM)
+ANY_SPEC = pl.BlockSpec(memory_space=pl.ANY)
+
+
+def attend(lengths, queries, entries, cache, residual, gain, n_chips):
     _, rows, width = queries.shape
     span = cache.shape[2]
     tiles = width // HD
-    whole = lambda *shape: pl.BlockSpec(shape, lambda i, *_: (0,) * len(shape))
-    by_head = lambda *shape: pl.BlockSpec(
-        shape, lambda i, head_ref, _: (0,) * (len(shape) - 1) + (head_ref[0],)
-    )
     return pl.pallas_call(
         attend_kernel,
-        grid_spec=pltpu.PrefetchScalarGridSpec(
-            num_scalar_prefetch=2,
-            grid=(1,),
-            in_specs=[
-                whole(2, rows, width),
-                by_head(2, 2, rows, HD),
-                by_head(2, rows, span, HD),
-                whole(2, rows, width),
-                whole(1, width),
-            ],
-            out_specs=[whole(n_chips, rows, width), whole((tiles + 1) * rows, HD)],
-        ),
+        in_specs=[HBM_SPEC] * 6,
+        out_specs=[VMEM_SPEC] * 2,
         out_shape=[
             jax.ShapeDtypeStruct((n_chips, rows, width), BF16),
             jax.ShapeDtypeStruct(((tiles + 1) * rows, HD), BF16),
         ],
-        compiler_params=pltpu.CompilerParams(vmem_limit_bytes=16 * 2**20),
+        scratch_shapes=[
+            pltpu.SMEM((rows,), jnp.int32),
+            pltpu.VMEM((2, rows, width), BF16),
+            pltpu.VMEM((2, 2, rows, HD), BF16),
+            pltpu.VMEM((2, rows, span, HD), BF16),
+            pltpu.VMEM((2, rows, width), BF16),
+            pltpu.VMEM((width,), BF16),
+            pltpu.SemaphoreType.DMA((6,)),
+        ],
+        compiler_params=pltpu.CompilerParams(vmem_limit_bytes=60 * 2**20),
         cost_estimate=pl.CostEstimate(flops=10**7, bytes_accessed=300_000, transcendentals=20_000),
-    )(head, lengths, queries, entries, cache, residual, gain)
+    )(lengths, queries, entries, cache, residual, gain)
 
 
 def product(pick, rows_all, mine, peer, extra, n_tp):
-    vmem = pl.BlockSpec(memory_space=pltpu.VMEM)
-    chips, per, _ = rows_all.shape
+    chips, per, width = rows_all.shape
     cols = mine.shape[2] // n_tp
-    lines = chips * per // 2 + extra.shape[0]
+    message = (n_tp, chips * per // 2 + extra.shape[0], 2 * cols)
+    step = 16 * cols
+    n_steps = n_tp * cols // step
     return pl.pallas_call(
         product_kernel,
-        in_specs=[pl.BlockSpec(memory_space=pltpu.SMEM), vmem, vmem, vmem, vmem],
-        out_specs=vmem,
-        out_shape=jax.ShapeDtypeStruct((n_tp, lines, 2 * cols), BF16),
-        compiler_params=pltpu.CompilerParams(vmem_limit_bytes=16 * 2**20),
+        in_specs=[pl.BlockSpec(memory_space=pltpu.SMEM), ANY_SPEC, HBM_SPEC, HBM_SPEC, ANY_SPEC],
+        out_specs=HBM_SPEC,
+        out_shape=jax.ShapeDtypeStruct(message, BF16),
+        scratch_shapes=[
+            pltpu.VMEM(rows_all.shape, BF16),
+            pltpu.VMEM(extra.shape, BF16),
+            pltpu.VMEM((n_steps, width, step), BF16),
+            pltpu.VMEM(message, BF16),
+            pltpu.SemaphoreType.DMA((n_steps + 2,)),
+            pltpu.SemaphoreType.DMA((n_steps,)),
+        ],
+        compiler_params=pltpu.CompilerParams(vmem_limit_bytes=60 * 2**20),
         cost_estimate=pl.CostEstimate(flops=13 * 10**7, bytes_accessed=3_000_000, transcendentals=0),
     )(pick, rows_all, mine, peer, extra)
 
@@ -171,10 +239,10 @@
     n_chips = n_rep // 2
     row_count, width = queries.shape[1], queries.shape[2]
     rep, tp = lax.axis_index("rep"), lax.axis_index("tp")
-    kv_head = (tp // (n_tp // KVH)).astype(jnp.int32).reshape(1)
     send, extra = attend(
-        kv_head, lengths, queries, new_entries, kv_cache, residual, norm_gain[None], n_chips
-    )
+        lengths, queries, new_entries, kv_cache, residual, norm_gain, n_chips
+    )
+    sectioning, send = lax.optimization_barrier((sectioning, send))
 
     same_core = [[i for i in range(n_rep) if i % 2 == core] for core in range(2)]
     rows_all = exchange(send, "rep", same_core)

time: 77.2 us -> 71.5 us (0.926)
  local copies, waits for them, and re-layouts: 7.85 us -> 2.03 us
    unnamed x14 -> x4, local copies, waits for them, and re-layouts: 5.75 us -> 0.62 us
  transfers between devices with their start and end apart: 4 -> 4, of which waited for: 3 -> 3; matrix products, arithmetic and copies ran while one was open for 3% -> 3% of each run, Pallas kernels for 2% -> 0%
where the time goes in v3:
time: 71.5 us; the launch traced here: 71 us
  waiting for transfers between devices  35.2 us (49%)
  starting transfers between devices  26.2 us (37%)
  Pallas kernels  4.17 us (6%)
  local copies, waits for them, and re-layouts  2.03 us (3%)
  other arithmetic  1.46 us (2%)
  between operations  1.38 us (2%)
    all_to_all x3, waiting for transfers between devices, exchange(): lax.all_to_all(chunks, axis, split_axis=0, concat_axis=0, axis_index_grou...  35.2 us
    all_to_all x3, starting transfers between devices, exchange(): lax.all_to_all(chunks, axis, split_axis=0, concat_axis=0, axis_index_grou...  24.3 us
    pallas_call x1, Pallas kernels, attend(): pl.pallas_call(attend_kernel, in_specs=[HBM_SPEC] * 6, out_specs=[VMEM_SP...  2.27 us
    ppermute x1, starting transfers between devices, body(): lax.ppermute(sectioning, 'rep', [(i, i ^ 1) for i in range(n_rep)])  1.92 us
    pallas_call x1, Pallas kernels, product(): pl.pallas_call(product_kernel, in_specs=[pl.BlockSpec(memory_space=pltpu....  1.9 us
  transfers between devices with their start and end apart: 4, of which 3 were waited for; matrix products, arithmetic and copies ran while one was open for 3% of the time, Pallas kernels for 0%

profile of v3, /device:TPU:64, one launch (start us, length us, event | category | flops | bytes accessed | tf_op | source)
XLA Modules:
  0.0 71.0 jit_solution(12386472358334354453)
XLA Ops:
  0.0 0.0 copy-start
  0.0 2.3 %shard_map.91 = (bf16[8,8,512]{2,1,0:T(8,128)(2,1)}, bf16[40,128]{1,0:T(8,128)(2,1)}) custom-call(s32[8]{0:T(128)} %lengths_hbm.1, bf16[2,8,512]{2,1,0:T(8,128)(2,1)} %q_hbm.1, bf16[2,2,8,1024]{3,2,1,0:T(8,128)(2,1)} %e_hbm.1, bf16[2,8,32,1024]{3,2,1,0:T(8,128)(2,1)} %kv_hbm.1, bf16[2,8,512]{2,1,0:T(8,128)(2,1)} %res_hbm.1, bf16[512]{0:T(512)(128)(2,1)} %gain_hbm.1), custom_call_target="tpu_custom_call" | custom-call | flops 10000000 | bytes 300000 | tf_op jit(solution)/shard_map/pallas_call | solution.py:189
  2.3 1.9 %collective-permute-start = (bf16[1,512,2048]{2,1,0:T(8,128)(2,1)}, bf16[1,512,2048]{2,1,0:T(8,128)(2,1)}, u32[]{:S(2)}, u32[]{:S(2)}) collective-permute-start(bf16[1,512,2048]{2,1,0:T(8,128)(2,1)} %mine_hbm), channel_id=1, source_target_pairs={{0,32},{32,0},{64,96},{96,64},{128,160},{160,128},{192,224},{224,1... | collective-permute-start | bytes 6291464 | tf_op jit(solution)/shard_map/ppermute | solution.py:249
  4.2 9.6 %all-to-all-start = ((bf16[8,8,512]{2,1,0:T(8,128)(2,1)}), bf16[8,8,512]{2,1,0:T(8,128)(2,1)S(1)}, u32[]{:S(2)}, u32[]{:S(2)}) async-start(bf16[8,8,512]{2,1,0:T(8,128)(2,1)} %get-tuple-element.10), calls=%async_computation | async-start | bytes 131072 | tf_op jit(solution)/shard_map/all_to_all | solution.py:17
  13.8 1.2 %dynamic_slice.3 = s32[1]{0:T(128)} dynamic-slice(s32[32]{0:T(128)} %param.16, s32[]{:T(128)S(6)} %select_n.24), dynamic_slice_sizes={1} | dynamic-slice | bytes 12 | tf_op jit(solution)/shard_map/dynamic_slice | solution.py:250
  16.3 7.7 %all-to-all-done.rows_hbm = bf16[8,8,512]{2,1,0:T(8,128)(2,1)S(1)} async-done(((bf16[8,8,512]{2,1,0:T(8,128)(2,1)}), bf16[8,8,512]{2,1,0:T(8,128)(2,1)S(1)}, u32[]{:S(2)}, u32[]{:S(2)}) %all-to-all-start) | async-done | bytes 65568 | tf_op jit(solution)/shard_map/all_to_all | solution.py:17
  24.0 0.0 copy-start.1
  24.0 0.0 collective-permute-done.peer_hbm
  24.0 0.6 copy-done.1
  24.7 1.9 %shard_map.92 = bf16[32,72,128]{2,1,0:T(8,128)(2,1)} custom-call(s32[1]{0:T(128)} %bitcast.1.pick_ref, bf16[8,8,512]{2,1,0:T(8,128)(2,1)} %copy-done.1, bf16[1,512,2048]{2,1,0:T(8,128)(2,1)} %mine_hbm, bf16[1,512,2048]{2,1,0:T(8,128)(2,1)} %collective-permute-done.peer_hbm, bf16[40,128]{1,0:T(8,128)(2,1)} %get-tuple-element.12.extra_hbm), custom_call_target="tpu_custom_call" | custom-call | flops 130000000 | bytes 3000000 | tf_op jit(solution)/shard_map/pallas_call | solution.py:217
  26.6 11.3 %all-to-all-start.1 = ((bf16[32,72,128]{2,1,0:T(8,128)(2,1)}), bf16[32,72,128]{2,1,0:T(8,128)(2,1)S(1)}, u32[]{:S(2)}, u32[]{:S(2)}) async-start(bf16[32,72,128]{2,1,0:T(8,128)(2,1)} %shard_map.92), calls=%async_computation.1 | async-start | bytes 1179648 | tf_op jit(solution)/shard_map/all_to_all | solution.py:17
  37.9 18.1 %all-to-all-done.1 = bf16[32,72,128]{2,1,0:T(8,128)(2,1)S(1)} async-done(((bf16[32,72,128]{2,1,0:T(8,128)(2,1)}), bf16[32,72,128]{2,1,0:T(8,128)(2,1)S(1)}, u32[]{:S(2)}, u32[]{:S(2)}) %all-to-all-start.1) | async-done | bytes 589856 | tf_op jit(solution)/shard_map/all_to_all | solution.py:17
  56.0 0.1 add_rsqrt_fusion
  56.1 0.2 slice_reduce_fusion.2
  56.3 0.1 fusion.3
  56.4 0.6 pad_maximum_fusion
  56.9 3.3 %all-to-all-start.2 = ((bf16[8,8,128]{2,1,0:T(8,128)(2,1)}), bf16[8,8,128]{2,1,0:T(8,128)(2,1)S(1)}, u32[]{:S(2)}, u32[]{:S(2)}) async-start(bf16[8,8,128]{2,1,0:T(8,128)(2,1)} %pad_maximum_fusion), calls=%async_computation.2 | async-start | bytes 32768 | tf_op jit(solution)/shard_map/all_to_all | solution.py:17
  60.3 0.0 copy-done
  60.3 0.6 fusion.1
  60.9 9.4 %all-to-all-done.2 = bf16[8,8,128]{2,1,0:T(8,128)(2,1)S(1)} async-done(((bf16[8,8,128]{2,1,0:T(8,128)(2,1)}), bf16[8,8,128]{2,1,0:T(8,128)(2,1)S(1)}, u32[]{:S(2)}, u32[]{:S(2)}) %all-to-all-start.2) | async-done | bytes 16416 | tf_op jit(solution)/shard_map/all_to_all | solution.py:17
  70.4 0.1 fusion.2
  70.4 0.6 pad_maximum_fusion.1
  (2 shorter events, 0.0 us)
Async XLA Ops:
  0.0 60.3 %copy-start = (bf16[16384,64]{0,1:T(8,128)(2,1)S(1)}, bf16[16384,64]{0,1:T(8,128)(2,1)}, u32[]{:S(2)}) copy-start(bf16[16384,64]{0,1:T(8,128)(2,1)} %param.14) | copy-start | bytes 6291460
  2.3 21.8 %collective-permute-start = (bf16[1,512,2048]{2,1,0:T(8,128)(2,1)}, bf16[1,512,2048]{2,1,0:T(8,128)(2,1)}, u32[]{:S(2)}, u32[]{:S(2)}) collective-permute-start(bf16[1,512,2048]{2,1,0:T(8,128)(2,1)} %mine_hbm), channel_id=1, source_target_pairs={{0,32},{32,0},{64,96},{96,64},{128,160},{160,128},{192,224},{224,1... | collective-permute-start | bytes 6291464 | tf_op jit(solution)/shard_map/ppermute | solution.py:249
  4.2 19.8 %all-to-all-start = ((bf16[8,8,512]{2,1,0:T(8,128)(2,1)}), bf16[8,8,512]{2,1,0:T(8,128)(2,1)S(1)}, u32[]{:S(2)}, u32[]{:S(2)}) async-start(bf16[8,8,512]{2,1,0:T(8,128)(2,1)} %get-tuple-element.10), calls=%async_computation | async-start | bytes 131072 | tf_op jit(solution)/shard_map/all_to_all | solution.py:17
  24.0 0.6 copy-start.1
  26.6 29.4 %all-to-all-start.1 = ((bf16[32,72,128]{2,1,0:T(8,128)(2,1)}), bf16[32,72,128]{2,1,0:T(8,128)(2,1)S(1)}, u32[]{:S(2)}, u32[]{:S(2)}) async-start(bf16[32,72,128]{2,1,0:T(8,128)(2,1)} %shard_map.92), calls=%async_computation.1 | async-start | bytes 1179648 | tf_op jit(solution)/shard_map/all_to_all | solution.py:17
  56.9 13.4 %all-to-all-start.2 = ((bf16[8,8,128]{2,1,0:T(8,128)(2,1)}), bf16[8,8,128]{2,1,0:T(8,128)(2,1)S(1)}, u32[]{:S(2)}, u32[]{:S(2)}) async-start(bf16[8,8,128]{2,1,0:T(8,128)(2,1)} %pad_maximum_fusion), calls=%async_computation.2 | async-start | bytes 32768 | tf_op jit(solution)/shard_map/all_to_all | solution.py:17

commit v4 on v3

--- a/solution.py
+++ b/solution.py
@@ -20,7 +20,7 @@
 
 
 def attend_kernel(
-    lengths_hbm, q_hbm, e_hbm, kv_hbm, res_hbm, gain_hbm, send_ref, extra_ref,
+    lengths_hbm, q_hbm, e_hbm, kv_hbm, res_hbm, gain_hbm, send_ref,
     lengths_ref, q_ref, e_ref, kv_ref, res_ref, gain_ref, sems,
 ):
     head = lax.div(lax.axis_index("tp"), lax.div(lax.axis_size("tp"), KVH))
@@ -76,37 +76,39 @@
     attended = jnp.dot(weights, keys(1), preferred_element_type=F32)
 
     lane = lax.broadcasted_iota(jnp.int32, (rows, HD), 1)
-    pieces = jnp.zeros((rows, HD), F32)
     gain = gain_ref[...].astype(F32)[None]
+    gained, squares = [], []
     for s in range(2):
         base = s * tiles * rows
         there = jnp.concatenate(
             [attended[base + t * rows : base + (t + 1) * rows] for t in range(tiles)], axis=1
         )
         stream = res_ref[s].astype(F32) + there
-        square = jnp.sum(stream * stream, axis=1, keepdims=True)
-        high = square.astype(BF16).astype(F32)
-        pieces = jnp.where(lane == s, high, jnp.where(lane == 2 + s, square - high, pieces))
-        gained = stream * gain
-        if s == 0:
-            first = stacked(gained)
-        else:
-            gained = gained.astype(BF16)
-            for p in range(send_ref.shape[0]):
-                send_ref[p] = gained
-    extra_ref[...] = jnp.concatenate([first, pieces], axis=0).astype(BF16)
+        squares.append(jnp.sum(stream * stream, axis=1, keepdims=True))
+        gained.append(stream * gain)
+    spot = lane % (HD // 2)
+    pieces = jnp.zeros((rows, HD), F32)
+    for s in range(2):
+        high = squares[s].astype(BF16).astype(F32)
+        pieces = jnp.where(
+            spot == s, high, jnp.where(spot == 2 + s, squares[s] - high, pieces)
+        )
+    second = gained[1].astype(BF16)
+    for p in range(send_ref.shape[0]):
+        tile = gained[0][:, p // 2 * HD : (p // 2 + 1) * HD]
+        own = (lane >= HD // 2) if p % 2 else (lane < HD // 2)
+        send_ref[p, :, : tiles * HD] = second
+        send_ref[p, :, tiles * HD :] = jnp.where(own, tile, pieces).astype(BF16)
 
 
 def product_kernel(
-    pick_ref, rows_hbm, mine_hbm, peer_hbm, extra_hbm, out_hbm,
-    rows_ref, extra_ref, weight_ref, out_ref, in_sems, out_sems,
+    pick_ref, rows_hbm, mine_hbm, peer_hbm, out_hbm,
+    rows_ref, weight_ref, out_ref, in_sems, out_sems,
 ):
-    n_tp = out_ref.shape[0]
+    n_tp, chips, per, _ = out_ref.shape
     cols = mine_hbm.shape[2] // n_tp
-    chips, per, width = rows_ref.shape
+    n_steps, width, step = weight_ref.shape
     count = chips * per
-    half = count // 2
-    n_steps, _, step = weight_ref.shape
     each = n_tp // n_steps
     pick = pick_ref[0]
 
@@ -119,12 +121,8 @@
         part = pl.ds(i * each, each)
         return pltpu.make_async_copy(out_ref.at[part], out_hbm.at[part], out_sems.at[i])
 
-    small = [
-        pltpu.make_async_copy(extra_hbm, extra_ref, in_sems.at[n_steps]),
-        pltpu.make_async_copy(rows_hbm, rows_ref, in_sems.at[n_steps + 1]),
-    ]
-    for copy in small:
-        copy.start()
+    small = pltpu.make_async_copy(rows_hbm, rows_ref, in_sems.at[n_steps])
+    small.start()
 
     @pl.when(pick == 0)
     def _():
@@ -136,14 +134,16 @@
         for i in range(n_steps):
             fetch(peer_hbm, i).start()
 
-    for copy in small:
-        copy.wait()
-    extra = extra_ref[...].astype(F32)
+    small.wait()
 
     @pl.when(pick < 2)
     def _():
-        low = lax.broadcasted_iota(jnp.int32, (half, 2 * cols), 1) < cols
-        rows = rows_ref[...].reshape(count, width)
+        rows = rows_ref[:, :, :width].reshape(count, width)
+        other = rows_ref[:, :, width:].astype(F32).reshape(count, 2 * cols)
+        right = lax.broadcasted_iota(jnp.int32, (count, 2 * cols), 1) >= cols
+        odd_place = lax.rem(lax.div(lax.axis_index("rep"), 2), 2) == 1
+        odd_lanes = jnp.full((count, 2 * cols), jnp.where(odd_place, 1, 0)) == 1
+        features = jnp.where(right, 1, 0) == jnp.where(odd_place, 1, 0)
 
         def one(i, carry):
             fetch(mine_hbm, i).wait()
@@ -151,11 +151,12 @@
             for j in range(each // 2):
                 tile = part[:, j * 2 * cols : (j + 1) * 2 * cols]
                 turned = pltpu.roll(tile, cols, 1)
-                even = jnp.where(low, tile[:half], turned[half:])
-                odd = jnp.where(low, turned[:half], tile[half:])
+                left_block = jnp.where(odd_lanes, tile, turned)
+                right_block = jnp.where(odd_lanes, turned, tile)
                 at = i * each + 2 * j
-                out_ref[at] = jnp.concatenate([even, extra], axis=0).astype(BF16)
-                out_ref[at + 1] = jnp.concatenate([odd, extra], axis=0).astype(BF16)
+                for k, block in enumerate((left_block, right_block)):
+                    block = jnp.where(features, other, block)
+                    out_ref[at + k] = block.reshape(chips, per, 2 * cols).astype(BF16)
             ship(i).start()
             return carry
 
@@ -163,10 +164,10 @@
 
     @pl.when(pick > 1)
     def _():
-        empty = jnp.concatenate([jnp.zeros((half, 2 * cols), F32), extra], axis=0).astype(BF16)
+        same = rows_ref[:, :, width:]
 
         def one(at, carry):
-            out_ref[at] = empty
+            out_ref[at] = same
             return carry
 
         lax.fori_loop(0, n_tp, one, 0)
@@ -185,15 +186,11 @@
 def attend(lengths, queries, entries, cache, residual, gain, n_chips):
     _, rows, width = queries.shape
     span = cache.shape[2]
-    tiles = width // HD
     return pl.pallas_call(
         attend_kernel,
         in_specs=[HBM_SPEC] * 6,
-        out_specs=[VMEM_SPEC] * 2,
-        out_shape=[
-            jax.ShapeDtypeStruct((n_chips, rows, width), BF16),
-            jax.ShapeDtypeStruct(((tiles + 1) * rows, HD), BF16),
-        ],
+        out_specs=VMEM_SPEC,
+        out_shape=jax.ShapeDtypeStruct((n_chips, rows, width + HD), BF16),
         scratch_shapes=[
             pltpu.SMEM((rows,), jnp.int32),
             pltpu.VMEM((2, rows, width), BF16),
@@ -208,28 +205,28 @@
     )(lengths, queries, entries, cache, residual, gain)
 
 
-def product(pick, rows_all, mine, peer, extra, n_tp):
-    chips, per, width = rows_all.shape
+def product(pick, rows_all, mine, peer, n_tp):
+    chips, per, _ = rows_all.shape
+    width = mine.shape[1]
     cols = mine.shape[2] // n_tp
-    message = (n_tp, chips * per // 2 + extra.shape[0], 2 * cols)
+    message = (n_tp, chips, per, 2 * cols)
     step = 16 * cols
     n_steps = n_tp * cols // step
     return pl.pallas_call(
         product_kernel,
-        in_specs=[pl.BlockSpec(memory_space=pltpu.SMEM), ANY_SPEC, HBM_SPEC, HBM_SPEC, ANY_SPEC],
+        in_specs=[pl.BlockSpec(memory_space=pltpu.SMEM), ANY_SPEC, HBM_SPEC, HBM_SPEC],
         out_specs=HBM_SPEC,
         out_shape=jax.ShapeDtypeStruct(message, BF16),
         scratch_shapes=[
             pltpu.VMEM(rows_all.shape, BF16),
-            pltpu.VMEM(extra.shape, BF16),
             pltpu.VMEM((n_steps, width, step), BF16),
             pltpu.VMEM(message, BF16),
-            pltpu.SemaphoreType.DMA((n_steps + 2,)),
+            pltpu.SemaphoreType.DMA((n_steps + 1,)),
             pltpu.SemaphoreType.DMA((n_steps,)),
         ],
         compiler_params=pltpu.CompilerParams(vmem_limit_bytes=60 * 2**20),
         cost_estimate=pl.CostEstimate(flops=13 * 10**7, bytes_accessed=3_000_000, transcendentals=0),
-    )(pick, rows_all, mine, peer, extra)
+    )(pick, rows_all, mine, peer)
 
 
 def body(
@@ -238,10 +235,9 @@
     n_rep, n_tp = lax.axis_size("rep"), lax.axis_size("tp")
     n_chips = n_rep // 2
     row_count, width = queries.shape[1], queries.shape[2]
+    cols = serving.shape[1]
     rep, tp = lax.axis_index("rep"), lax.axis_index("tp")
-    send, extra = attend(
-        lengths, queries, new_entries, kv_cache, residual, norm_gain, n_chips
-    )
+    send = attend(lengths, queries, new_entries, kv_cache, residual, norm_gain, n_chips)
     sectioning, send = lax.optimization_barrier((sectioning, send))
 
     same_core = [[i for i in range(n_rep) if i % 2 == core] for core in range(2)]
@@ -249,26 +245,27 @@
     peer_rows = lax.ppermute(sectioning, "rep", [(i, i ^ 1) for i in range(n_rep)])
     owner = owner_map[tp]
     pick = jnp.where(owner == rep, 0, jnp.where(owner == (rep ^ 1), 1, 2))
-    message = product(
-        pick.astype(jnp.int32).reshape(1), rows_all, sectioning, peer_rows, extra, n_tp
-    )
-
-    half = n_chips * row_count // 2
-    tiles = width // HD
-    got = exchange(message, "tp")
-    cols = sectioning.shape[2] // n_tp
-    summed = jnp.sum(got[:, :half].astype(F32), axis=0).astype(BF16)
-    summed = summed.reshape(n_chips // 2, row_count, 2 * cols)
-    mine = exchange(jnp.concatenate([summed, summed], axis=0), "rep", same_core)
-    second = jnp.sum(mine.astype(F32), axis=0)
-    second = jnp.where(rep // 2 < n_chips // 2, second[:, :cols], second[:, cols:])
-
-    parts = jnp.sum(got[:, half + tiles * row_count :, :4].astype(F32), axis=0)
-    mean_square = (parts[:, :2] + parts[:, 2:]) / F32(D)
-    scale = lax.rsqrt(mean_square + 1e-05)
-    features = got[:, half : half + tiles * row_count].reshape(n_tp, tiles, row_count, HD)
+    message = product(pick.astype(jnp.int32).reshape(1), rows_all, sectioning, peer_rows, n_tp)
+
+    everyone = [[r * n_tp + t for t in range(n_tp) for r in replicas] for replicas in same_core]
+    got = exchange(
+        message.reshape(n_tp * n_chips, row_count, 2 * cols), ("rep", "tp"), everyone
+    ).reshape(n_tp, n_chips // 2, 2, row_count, 2 * cols)
+    left = jnp.arange(2 * cols, dtype=jnp.int32)[None, None, None, :] < cols
+    features = jnp.where(left, got[:, :, 0], got[:, :, 1])
     features = features.transpose(2, 0, 1, 3).reshape(row_count, n_tp * width)
     first = jnp.dot(features, serving, preferred_element_type=F32)
+
+    mixed = jnp.where(left, got[:, :, 1], got[:, :, 0]).astype(F32)
+    pair = jnp.arange(n_chips // 2, dtype=jnp.int32)[None, :, None, None]
+    source = 2 * pair + jnp.where(left, 1, 0)
+    chip = (owner_map // 2)[:, None, None, None]
+    second = jnp.sum(jnp.where(chip == source, mixed, F32(0)), axis=(0, 1))
+    second = second[:, :cols] + second[:, cols:]
+    squares = jnp.sum(jnp.where((chip ^ 1) == source, mixed, F32(0)), axis=(0, 1))
+    squares = squares[:, :cols] + squares[:, cols:]
+    mean_square = (squares[:, :2] + squares[:, 2:4]) / F32(D)
+    scale = lax.rsqrt(mean_square + 1e-05)
     return jnp.stack([first * scale[:, :1], second * scale[:, 1:]]).astype(BF16)
 
 

time: 71.5 us -> 64.9 us (0.908)
  the two profiles are of different devices: /device:TPU:64 before, /device:TPU:16 now
where the time goes in v4:
time: 64.9 us; the launch traced here: 64.5 us
  starting transfers between devices  27.6 us (43%)
  waiting for transfers between devices  27.3 us (42%)
  Pallas kernels  4.21 us (6%)
  local copies, waits for them, and re-layouts  2.05 us (3%)
  between operations  1.4 us (2%)
  other arithmetic  1.32 us (2%)
  matrix products  0.66 us (1%)
    all_to_all x2, waiting for transfers between devices, exchange(): lax.all_to_all(chunks, axis, split_axis=0, concat_axis=0, axis_index_grou...  27.3 us
    all_to_all x2, starting transfers between devices, exchange(): lax.all_to_all(chunks, axis, split_axis=0, concat_axis=0, axis_index_grou...  25.6 us
    pallas_call x1, Pallas kernels, attend(): pl.pallas_call(attend_kernel, in_specs=[HBM_SPEC] * 6, out_specs=VMEM_SPE...  2.31 us
    ppermute x1, starting transfers between devices, body(): lax.ppermute(sectioning, 'rep', [(i, i ^ 1) for i in range(n_rep)])  1.92 us
    pallas_call x1, Pallas kernels, product(): pl.pallas_call(product_kernel, in_specs=[pl.BlockSpec(memory_space=pltpu....  1.91 us
  transfers between devices with their start and end apart: 3, of which 2 were waited for; matrix products, arithmetic and copies ran while one was open for 2% of the time, Pallas kernels for 0%

profile of v4, /device:TPU:16, one launch (start us, length us, event | category | flops | bytes accessed | tf_op | source)
XLA Modules:
  0.0 64.5 jit_solution(18391624307297502411)
XLA Ops:
  0.0 0.0 copy-start
  0.0 2.3 %shard_map.91 = bf16[8,8,640]{2,1,0:T(8,128)(2,1)} custom-call(s32[8]{0:T(128)} %lengths_hbm.1, bf16[2,8,512]{2,1,0:T(8,128)(2,1)} %q_hbm.1, bf16[2,2,8,1024]{3,2,1,0:T(8,128)(2,1)} %e_hbm.1, bf16[2,8,32,1024]{3,2,1,0:T(8,128)(2,1)} %kv_hbm.1, bf16[2,8,512]{2,1,0:T(8,128)(2,1)} %res_hbm.1, bf16[512]{0:T(512)(128)(2,1)} %gain_hbm.1), custom_call_target="tpu_custom_call" | custom-call | flops 10000000 | bytes 300000 | tf_op jit(solution)/shard_map/pallas_call | solution.py:189
  2.3 1.9 %collective-permute-start = (bf16[1,512,2048]{2,1,0:T(8,128)(2,1)}, bf16[1,512,2048]{2,1,0:T(8,128)(2,1)}, u32[]{:S(2)}, u32[]{:S(2)}) collective-permute-start(bf16[1,512,2048]{2,1,0:T(8,128)(2,1)} %mine_hbm), channel_id=1, source_target_pairs={{0,32},{32,0},{64,96},{96,64},{128,160},{160,128},{192,224},{224,1... | collective-permute-start | bytes 6291464 | tf_op jit(solution)/shard_map/ppermute | solution.py:245
  4.2 7.8 %all-to-all-start = ((bf16[8,8,640]{2,1,0:T(8,128)(2,1)}), bf16[8,8,640]{2,1,0:T(8,128)(2,1)S(1)}, u32[]{:S(2)}, u32[]{:S(2)}) async-start(bf16[8,8,640]{2,1,0:T(8,128)(2,1)} %shard_map.91), calls=%async_computation | async-start | bytes 163840 | tf_op jit(solution)/shard_map/all_to_all | solution.py:17
  12.0 1.2 %dynamic_slice.3 = s32[1]{0:T(128)} dynamic-slice(s32[32]{0:T(128)} %param.16, s32[]{:T(128)S(6)} %select_n.41), dynamic_slice_sizes={1} | dynamic-slice | bytes 12 | tf_op jit(solution)/shard_map/dynamic_slice | solution.py:246
  14.6 7.8 %all-to-all-done.rows_hbm = bf16[8,8,640]{2,1,0:T(8,128)(2,1)S(1)} async-done(((bf16[8,8,640]{2,1,0:T(8,128)(2,1)}), bf16[8,8,640]{2,1,0:T(8,128)(2,1)S(1)}, u32[]{:S(2)}, u32[]{:S(2)}) %all-to-all-start) | async-done | bytes 81952 | tf_op jit(solution)/shard_map/all_to_all | solution.py:17
  22.3 0.0 copy-start.1
  22.3 0.0 collective-permute-done.peer_hbm
  22.3 0.6 copy-done.1
  23.0 0.0 copy-start.2
  23.0 1.9 %shard_map.92 = bf16[32,8,8,128]{3,2,1,0:T(8,128)(2,1)} custom-call(s32[1]{0:T(128)} %bitcast.1.pick_ref, bf16[8,8,640]{2,1,0:T(8,128)(2,1)} %copy-done.1, bf16[1,512,2048]{2,1,0:T(8,128)(2,1)} %mine_hbm, bf16[1,512,2048]{2,1,0:T(8,128)(2,1)} %collective-permute-done.peer_hbm), custom_call_target="tpu_custom_call" | custom-call | flops 130000000 | bytes 3000000 | tf_op jit(solution)/shard_map/pallas_call | solution.py:215
  24.9 17.9 %all-to-all-start.1 = ((bf16[256,8,128]{2,1,0:T(8,128)(2,1)}), bf16[256,8,128]{2,1,0:T(8,128)(2,1)S(1)}, u32[]{:S(2)}, u32[]{:S(2)}) async-start(bf16[256,8,128]{2,1,0:T(8,128)(2,1)} %bitcast.37), calls=%async_computation.1 | async-start | bytes 1048576 | tf_op jit(solution)/shard_map/all_to_all | solution.py:17
  42.8 0.0 copy-done.2
  42.8 0.1 broadcast_add_fusion
  42.9 0.1 broadcast_compare_fusion
  43.0 19.6 %all-to-all-done.1 = bf16[256,8,128]{2,1,0:T(8,128)(2,1)S(1)} async-done(((bf16[256,8,128]{2,1,0:T(8,128)(2,1)}), bf16[256,8,128]{2,1,0:T(8,128)(2,1)S(1)}, u32[]{:S(2)}, u32[]{:S(2)}) %all-to-all-start.1) | async-done | bytes 524320 | tf_op jit(solution)/shard_map/all_to_all | solution.py:17
  62.6 0.2 fusion.2
  62.8 0.1 slice_add_fusion
  62.9 0.1 add_rsqrt_fusion
  63.0 0.2 slice_reduce_fusion.1
  63.2 0.1 fusion.4
  63.3 0.0 copy-done
  63.3 0.7 %fusion.1 = bf16[1,8,64]{2,1,0:T(8,128)(2,1)S(1)} fusion(bf16[8,16384]{1,0:T(8,128)(2,1)S(1)} %bitcast.38, bf16[16384,64]{0,1:T(8,128)(2,1)S(1)} %copy-done, f32[8]{0:T(128)S(1)} %get-tuple-element.11), kind=kOutput, calls=%fused_computation.2 | convolution fusion | flops 16778240 | bytes 2360352 | tf_op jit(solution)/shard_map/dot_general | solution.py:257
  63.9 0.6 pad_maximum_fusion
  (5 shorter events, 0.1 us)
Async XLA Ops:
  0.0 63.3 %copy-start = (bf16[16384,64]{0,1:T(8,128)(2,1)S(1)}, bf16[16384,64]{0,1:T(8,128)(2,1)}, u32[]{:S(2)}) copy-start(bf16[16384,64]{0,1:T(8,128)(2,1)} %param.14) | copy-start | bytes 6291460
  2.3 20.0 %collective-permute-start = (bf16[1,512,2048]{2,1,0:T(8,128)(2,1)}, bf16[1,512,2048]{2,1,0:T(8,128)(2,1)}, u32[]{:S(2)}, u32[]{:S(2)}) collective-permute-start(bf16[1,512,2048]{2,1,0:T(8,128)(2,1)} %mine_hbm), channel_id=1, source_target_pairs={{0,32},{32,0},{64,96},{96,64},{128,160},{160,128},{192,224},{224,1... | collective-permute-start | bytes 6291464 | tf_op jit(solution)/shard_map/ppermute | solution.py:245
  4.2 18.1 %all-to-all-start = ((bf16[8,8,640]{2,1,0:T(8,128)(2,1)}), bf16[8,8,640]{2,1,0:T(8,128)(2,1)S(1)}, u32[]{:S(2)}, u32[]{:S(2)}) async-start(bf16[8,8,640]{2,1,0:T(8,128)(2,1)} %shard_map.91), calls=%async_computation | async-start | bytes 163840 | tf_op jit(solution)/shard_map/all_to_all | solution.py:17
  22.3 0.6 copy-start.1
  23.0 19.8 %copy-start.2 = (s32[32]{0:T(128)S(1)}, s32[32]{0:T(128)}, u32[]{:S(2)}) copy-start(s32[32]{0:T(128)} %param.16) | copy-start | bytes 388
  24.9 37.7 %all-to-all-start.1 = ((bf16[256,8,128]{2,1,0:T(8,128)(2,1)}), bf16[256,8,128]{2,1,0:T(8,128)(2,1)S(1)}, u32[]{:S(2)}, u32[]{:S(2)}) async-start(bf16[256,8,128]{2,1,0:T(8,128)(2,1)} %bitcast.37), calls=%async_computation.1 | async-start | bytes 1048576 | tf_op jit(solution)/shard_map/all_to_all | solution.py:17
